TPU v7x, 512 devices: a whole 4x4x16 slice. The times are simulated.
512 devices in a mesh: dom: 64 (over x, z), rep: 8 (over y, core).
Axes of the slice: x: 4, y: 4, z: 16, core: 2. Of those that a mesh axis runs over, the one named last changes fastest.
Arguments:
- history: bfloat16 [2, 524288, 256], P(None, ('dom', 'rep')), may hold values from -6 to 6
- tile_values: bfloat16 [4096, 8, 128, 128], P(('dom', 'rep')), may hold values from -0.5 to 0.5
- tile_cols: int32 [4096, 8], P(('dom', 'rep')), may hold values from 0 to 11, all different within a row
- send_rows: int32 [512, 64, 8], P(('dom', 'rep')), may hold values from 0 to 1023
- send_count: int32 [512, 64], P(('dom', 'rep')), may hold values from 1 to 8, as said below
- node_ids: int32 [512, 1024], P(('dom', 'rep')), may hold values from 0 to 1023, each once within a row
- weights: bfloat16 [2, 256, 256], replicated, may hold values from -0.375 to 0.375
- upstream: bfloat16 [524288, 256], P(('dom', 'rep'))
Outputs:
- history_out: bfloat16 [1, 524288, 256], P(None, ('dom', 'rep'))
- weight_grads: float32 [2, 256, 256], replicated
Inputs may be any that keep to these rules, and one draw needn't show every extreme that they name: In each list the first send_count entries are live and the rest empty; in every draw each device has a list of 8 live entries. `tile_cols`: each row block names 8 different column blocks; blocks below 8 hold batch rows, the others halo slots.
All inputs are finite; a program needn't handle non-finite values.
Results may differ from a plain program's by a relative error of at most 0.0065.
Values may be sent and summed in bfloat16 or wider, within the bound.
A program may use at most 64 MiB of HBM per device.

v0:
```python
import math

import jax
import jax.numpy as jnp
from jax import lax
from jax.sharding import PartitionSpec as P

RESTART = 0.1


def layer_beta(level):
    return math.log(0.5 / (level + 1) + 1.0)


def silu_slope(preact):
    sigma = jax.nn.sigmoid(preact)
    return sigma * (1.0 + preact * (1.0 - sigma))


def outgoing(layer_table, send_rows, send_count):
    picked = jnp.take(layer_table, send_rows[0], axis=0)
    slot_index = lax.broadcasted_iota(jnp.int32, send_rows.shape[1:], 1)
    live_mask = slot_index < send_count[0][:, None]
    return jnp.where(live_mask[:, :, None], picked, jnp.zeros_like(picked))


def aggregate(tiles, tile_cols, node_table):
    tile_size = tiles.shape[2]
    blocks = node_table.reshape(-1, tile_size, node_table.shape[1])
    picked = jnp.take(blocks, tile_cols, axis=0)
    summed = jnp.einsum("rtij,rtjf->rif", tiles, picked, preferred_element_type=jnp.float32)
    return summed.reshape(-1, node_table.shape[1])


def spread_back(tiles, tile_cols, back_rows, batch_rows):
    tile_size = tiles.shape[2]
    blocks = back_rows.reshape(-1, tile_size, back_rows.shape[1])
    pieces = jnp.einsum("rtij,rif->rtjf", tiles, blocks, preferred_element_type=jnp.float32)
    targets = lax.broadcasted_iota(jnp.int32, (1, 1, batch_rows // tile_size), 2)
    owners = (tile_cols[:, :, None] == targets).astype(jnp.float32)
    placed = jnp.einsum("rtc,rtjf->cjf", owners, pieces, precision=lax.Precision.HIGHEST)
    return placed.reshape(batch_rows, back_rows.shape[1])


def local(history, tile_values, tile_cols, send_rows, send_count, node_ids, weights, upstream):
    levels = history.shape[0]
    batch_rows = history.shape[1]
    feature_width = history.shape[2]
    node_rows = node_ids[0]
    h_start = jnp.take(history[0], node_rows, axis=0)
    halos = [
        lax.all_to_all(
            outgoing(history[level], send_rows, send_count),
            "dom",
            split_axis=0,
            concat_axis=0,
            tiled=True,
        ).reshape(-1, feature_width)
        for level in range(levels)
    ]
    current = h_start
    mixed_all = []
    preact_all = []
    written = []
    for level in range(levels):
        node_table = jnp.concatenate([current, halos[level]], axis=0)
        summed = aggregate(tile_values, tile_cols, node_table)
        mixed_rows = ((1.0 - RESTART) * summed + RESTART * h_start.astype(jnp.float32)).astype(
            jnp.bfloat16
        )
        beta_value = layer_beta(level)
        preact = (1.0 - beta_value) * mixed_rows.astype(jnp.float32) + beta_value * jnp.dot(
            mixed_rows, weights[level], preferred_element_type=jnp.float32
        )
        current = jax.nn.silu(preact).astype(jnp.bfloat16)
        mixed_all.append(mixed_rows)
        preact_all.append(preact)
        if level + 1 < levels:
            written.append(
                jnp.zeros((batch_rows, feature_width), jnp.bfloat16).at[node_rows].set(current)
            )
    grads = [None] * levels
    grad_rows = (upstream.astype(jnp.float32) * silu_slope(preact_all[-1])).astype(jnp.bfloat16)
    for level in reversed(range(levels)):
        beta_value = layer_beta(level)
        local_grad = beta_value * jnp.dot(
            mixed_all[level].T, grad_rows, preferred_element_type=jnp.float32
        )
        grads[level] = local_grad
        if level > 0:
            back_rows = (
                (1.0 - beta_value) * grad_rows.astype(jnp.float32)
                + beta_value
                * jnp.dot(grad_rows, weights[level].T, preferred_element_type=jnp.float32)
            ).astype(jnp.bfloat16)
            delta = (1.0 - RESTART) * spread_back(tile_values, tile_cols, back_rows, batch_rows)
            grad_rows = (delta * silu_slope(preact_all[level - 1])).astype(jnp.bfloat16)
    stacked = jnp.stack(grads)
    stacked = lax.psum(stacked, ("dom", "rep"))
    nodes_all = batch_rows * lax.axis_size("dom") * lax.axis_size("rep")
    return (jnp.stack(written), stacked * (1.0 / math.sqrt(nodes_all)))


def solution(mesh):
    return jax.shard_map(
        local,
        mesh=mesh,
        in_specs=(
            P(None, ("dom", "rep"), None),
            P(("dom", "rep"), None, None, None),
            P(("dom", "rep"), None),
            P(("dom", "rep"), None, None),
            P(("dom", "rep"), None),
            P(("dom", "rep"), None),
            P(),
            P(("dom", "rep"), None),
        ),
        out_specs=(P(None, ("dom", "rep"), None), P()),
        check_vma=False,
    )
```

profile of v0, /device:TPU:1, one launch (start us, length us, event | category | flops | bytes accessed | tf_op | source)
XLA Modules:
  0.0 560.0 jit_solution(8905946658000197402)
XLA Ops:
  7.2 0.7 compare_and_fusion.1
  7.9 0.7 compare_select_fusion.2
  8.7 0.7 iota_compare_fusion.1
  9.6 1.3 slice_bitcast_fusion
  10.9 2.0 gather_fusion.3
  12.9 2.0 gather_fusion.1
  14.8 1.0 fusion.39
  15.8 19.1 %all-to-all-start = ((bf16[64,8,256]{2,1,0:T(8,128)(2,1)}), bf16[64,8,256]{2,1,0:T(8,128)(2,1)S(1)}, u32[]{:S(2)}, u32[]{:S(2)}) async-start(bf16[64,8,256]{2,1,0:T(8,128)(2,1)} %get-tuple-element.7), calls=%async_computation | async-start | bytes 524288 | tf_op jit(solution)/shard_map/all_to_all | solution.py:52
  35.1 3.9 gather_fusion
  39.0 2.9 copy.20
  42.2 11.8 %all-to-all-done = bf16[64,8,256]{2,1,0:T(8,128)(2,1)S(1)} async-done(((bf16[64,8,256]{2,1,0:T(8,128)(2,1)}), bf16[64,8,256]{2,1,0:T(8,128)(2,1)S(1)}, u32[]{:S(2)}, u32[]{:S(2)}) %all-to-all-start) | async-done | bytes 262176 | tf_op jit(solution)/shard_map/all_to_all | solution.py:52
  54.0 7.9 %all-to-all-start.1 = ((bf16[64,8,256]{2,1,0:T(8,128)(2,1)}), bf16[64,8,256]{2,1,0:T(8,128)(2,1)}, u32[]{:S(2)}, u32[]{:S(2)}) async-start(bf16[64,8,256]{2,1,0:T(8,128)(2,1)} %get-tuple-element.6), calls=%async_computation.1 | async-start | bytes 524288 | tf_op jit(solution)/shard_map/all_to_all | solution.py:52
  62.2 2.8 gather_fusion.2
  64.9 3.0 fusion.38
  68.2 0.8 copy-done.4
  69.0 1.6 multiply_convert_fusion.1
  70.6 9.2 %all-to-all-done.1 = bf16[64,8,256]{2,1,0:T(8,128)(2,1)} async-done(((bf16[64,8,256]{2,1,0:T(8,128)(2,1)}), bf16[64,8,256]{2,1,0:T(8,128)(2,1)}, u32[]{:S(2)}, u32[]{:S(2)}) %all-to-all-start.1) | async-done | bytes 262176 | tf_op jit(solution)/shard_map/all_to_all | solution.py:52
  79.9 1.2 pad_maximum_fusion.1
  81.0 2.8 gather_fusion.4
  83.8 3.0 fusion.37
  87.1 0.7 multiply_convert_fusion
  87.8 0.3 fusion.32
  88.7 1.2 fusion.54
  90.0 5.6 fusion.28
  95.5 0.3 copy.17
  95.9 0.3 fusion.36
  96.2 0.3 copy-done.5
  96.6 0.3 fusion.33
  96.9 0.8 pad_maximum_fusion.2
  97.8 6.1 %scatter_custom_fusion = bf16[1024,256]{1,0:T(8,128)(2,1)} fusion(s32[1024]{0:T(1024)S(1)} %bitcast.119, bf16[1024,256]{1,0:T(8,128)(2,1)} %get-tuple-element.10, bf16[]{:T(256)} %constant.29.clone.1), kind=kCustom, calls=%fused_computation.60 | custom fusion | bytes 524800 | tf_op jit(solution)/shard_map/scatter | solution.py:80
  103.9 447.4 %all-reduce.2.cloned.1.call-done = f32[2,256,256]{2,1,0:T(8,128)} async-done(((f32[2,256,256]{2,1,0:T(8,128)}), f32[2,256,256]{2,1,0:T(8,128)}) %all-reduce.2.cloned.1.call-update) | async-done | bytes 524304 | tf_op jit(solution)/shard_map/psum | solution.py:99
  551.2 1.9 broadcast_multiply_fusion
  (39 shorter events, 2.0 us)
Async XLA Ops:
  9.6 25.4 %copy-start.6 = (s32[8,8]{1,0:T(8,128)S(1)}, s32[8,8]{1,0:T(8,128)}, u32[]{:S(2)}) copy-start(s32[8,8]{1,0:T(8,128)} %param.14) | copy-start | bytes 772
  9.6 25.4 %copy-start.7 = (s32[1,1024]{1,0:T(1,128)S(1)}, s32[1,1024]{1,0:T(1,128)}, u32[]{:S(2)}) copy-start(s32[1,1024]{1,0:T(1,128)} %param.17) | copy-start | bytes 12292
  12.8 26.2 %copy-start = (bf16[8,8,128,128]{3,2,1,0:T(8,128)(2,1)S(1)}, bf16[8,8,128,128]{3,2,1,0:T(8,128)(2,1)}, u32[]{:S(2)}) copy-start(bf16[8,8,128,128]{3,2,1,0:T(8,128)(2,1)} %param.13) | copy-start | bytes 6291460
  15.8 38.2 %all-to-all-start = ((bf16[64,8,256]{2,1,0:T(8,128)(2,1)}), bf16[64,8,256]{2,1,0:T(8,128)(2,1)S(1)}, u32[]{:S(2)}, u32[]{:S(2)}) async-start(bf16[64,8,256]{2,1,0:T(8,128)(2,1)} %get-tuple-element.7), calls=%async_computation | async-start | bytes 524288 | tf_op jit(solution)/shard_map/all_to_all | solution.py:52
  54.0 25.9 %all-to-all-start.1 = ((bf16[64,8,256]{2,1,0:T(8,128)(2,1)}), bf16[64,8,256]{2,1,0:T(8,128)(2,1)}, u32[]{:S(2)}, u32[]{:S(2)}) async-start(bf16[64,8,256]{2,1,0:T(8,128)(2,1)} %get-tuple-element.6), calls=%async_computation.1 | async-start | bytes 524288 | tf_op jit(solution)/shard_map/all_to_all | solution.py:52
  61.9 489.4 %all-reduce.2.cloned.1.call-start = ((), (), s32[]{:S(2)}) async-start(), calls=%async_computation.2 | async-start | bytes 1048576 | tf_op jit(solution)/shard_map/psum | solution.py:99
  62.1 2.8 copy-start.1
  64.9 4.1 copy-start.9
  68.2 0.8 copy-start.4
  83.8 3.3 copy-start.8
  83.8 3.3 copy-start.10
  87.1 1.6 copy-start.2
  89.9 5.9 %copy-start.3 = (f32[1024,256]{1,0:T(8,128)S(1)}, f32[1024,256]{1,0:T(8,128)}, u32[]{:S(2)}) copy-start(f32[1024,256]{1,0:T(8,128)} %get-tuple-element.11) | copy-start | bytes 3145732
  95.5 1.1 copy-start.5
Sparse Core Ops, SparseCore 0:
  97.9 453.3 all-reduce.1
where the time goes:
time: 561 us; the launch traced here: 560 us
  waiting for transfers between devices  468 us (83%)
  starting transfers between devices  27.2 us (5%)
  local copies, waits for them, and re-layouts  25.8 us (5%)
  matrix products  16.1 us (3%)
  between operations  14.3 us (3%)
  other arithmetic  8.14 us (1%)
    psum x1, waiting for transfers between devices, local(): stacked = lax.psum(stacked, ('dom', 'rep'))  447 us
    all_to_all x2, starting transfers between devices, local(): lax.all_to_all(outgoing(history[level], send_rows, send_count), 'dom', sp...  27 us
    all_to_all x2, waiting for transfers between devices, local(): lax.all_to_all(outgoing(history[level], send_rows, send_count), 'dom', sp...  21 us
  transfers between devices with their start and end apart: 3, of which 3 were waited for; matrix products, arithmetic and copies ran while one was open for 4% of the time, Pallas kernels for 0%

commit v1 on v0

--- a/solution.py
+++ b/solution.py
@@ -1,11 +1,15 @@
+import functools
 import math
 
 import jax
 import jax.numpy as jnp
 from jax import lax
+from jax.experimental import pallas as pl
+from jax.experimental.pallas import tpu as pltpu
 from jax.sharding import PartitionSpec as P
 
 RESTART = 0.1
+RING = 16
 
 
 def layer_beta(level):
@@ -42,7 +46,159 @@
     return placed.reshape(batch_rows, back_rows.shape[1])
 
 
-def local(history, tile_values, tile_cols, send_rows, send_count, node_ids, weights, upstream):
+MESH = pl.DeviceIdType.MESH
+
+
+def span_wait(ref, sem):
+    pltpu.make_async_copy(ref, ref, sem).wait()
+
+
+def place(grid):
+    nx, ny, nz = grid
+    dom, rep = lax.axis_index("dom"), lax.axis_index("rep")
+    return dom // nz, dom % nz, rep // 2, rep % 2
+
+
+def plane_peer(grid, step):
+    nx, ny, nz = grid
+    x, z, y, core = place(grid)
+    other = (x * ny + y + step) % (nx * ny)
+    return ((other // ny) * nz + z, (other % ny) * 2 + core), other
+
+
+def ring_peer(grid, step):
+    nx, ny, nz = grid
+    x, z, y, core = place(grid)
+    other = (z + step) % nz
+    return (x * nz + other, y * 2 + core), other
+
+
+def greet_sum_peers(grid, barrier):
+    nx, ny, nz = grid
+    x, z, y, core = place(grid)
+
+    def signal(target):
+        pl.semaphore_signal(barrier, inc=1, device_id=target, device_id_type=MESH)
+
+    signal((x * nz + z, y * 2 + 1 - core))
+    lax.fori_loop(1, nx * ny, lambda step, c: (signal(plane_peer(grid, step)[0]), c)[1], 0)
+    lax.fori_loop(1, nz, lambda step, c: (signal(ring_peer(grid, step)[0]), c)[1], 0)
+
+
+def sum_body(grid, scale, grads, out, pair_src, pair_got, plane_src, plane_got, ring_src, ring_got, ring_all, plane_all, send_sems, recv_sems):
+    nx, ny, nz = grid
+    planes = nx * ny
+    x, z, y, core = place(grid)
+    partner = (x * nz + z, y * 2 + 1 - core)
+    mine = x * ny + y
+    rows = grads.shape[1] // planes
+    piece = rows // nz
+
+    def copy(stage, src, dst, target):
+        return pltpu.make_async_remote_copy(
+            src_ref=src, dst_ref=dst, send_sem=send_sems.at[stage], recv_sem=recv_sems.at[stage], device_id=target, device_id_type=MESH
+        )
+
+    pair_src[...] = grads[1 - core].astype(jnp.bfloat16)
+    hop = copy(0, pair_src, pair_got, partner)
+    hop.start()
+    hop.wait_recv()
+    plane_src[...] = (grads[core] + pair_got[...].astype(jnp.float32)).astype(jnp.bfloat16)
+
+    def plane_send(step, c):
+        target, other = plane_peer(grid, step)
+        start = pl.multiple_of(other * rows, rows)
+        copy(1, plane_src.at[pl.ds(start, rows)], plane_got.at[step - 1], target).start()
+        return c
+
+    lax.fori_loop(1, planes, plane_send, 0)
+    own = pl.multiple_of(mine * rows, rows)
+    total = grads[core, pl.ds(own, rows), :] + pair_got[pl.ds(own, rows), :].astype(jnp.float32)
+    span_wait(plane_got, recv_sems.at[1])
+    total = total + jnp.sum(plane_got[...].astype(jnp.float32), axis=0)
+    for part in range(nz):
+        ring_src[part] = total[part * piece : (part + 1) * piece]
+
+    def ring_send(step, c):
+        target, other = ring_peer(grid, step)
+        copy(2, ring_src.at[other], ring_got.at[step - 1], target).start()
+        return c
+
+    lax.fori_loop(1, nz, ring_send, 0)
+    part_sum = ring_src[z]
+    span_wait(ring_got, recv_sems.at[2])
+    for part in range(nz - 1):
+        part_sum = part_sum + ring_got[part]
+    ring_all[z] = part_sum * scale
+
+    def ring_share(step, c):
+        target, other = ring_peer(grid, step)
+        copy(3, ring_all.at[z], ring_all.at[z], target).start()
+        return c
+
+    lax.fori_loop(1, nz, ring_share, 0)
+    span_wait(ring_got, recv_sems.at[3])
+    summed = jnp.concatenate([ring_all[part] for part in range(nz)], axis=0)
+    plane_all[pl.ds(own, rows), :] = summed.astype(jnp.bfloat16)
+
+    def plane_share(step, c):
+        target, other = plane_peer(grid, step)
+        copy(4, plane_all.at[pl.ds(own, rows)], plane_all.at[pl.ds(own, rows)], target).start()
+        return c
+
+    lax.fori_loop(1, planes, plane_share, 0)
+    span_wait(plane_got, recv_sems.at[4])
+    back = copy(5, plane_all, out.at[core], partner)
+    back.start()
+    out[core] = plane_all[...]
+    back.wait_recv()
+    hop.wait_send()
+    span_wait(plane_got, send_sems.at[1])
+    span_wait(ring_got, send_sems.at[2])
+    span_wait(ring_got, send_sems.at[3])
+    span_wait(plane_got, send_sems.at[4])
+    back.wait_send()
+
+
+def sum_scratch(grid, side):
+    nx, ny, nz = grid
+    planes = nx * ny
+    rows = side // planes
+    piece = rows // nz
+    return [
+        pltpu.VMEM((side, side), jnp.bfloat16),
+        pltpu.VMEM((side, side), jnp.bfloat16),
+        pltpu.VMEM((side, side), jnp.bfloat16),
+        pltpu.VMEM((planes - 1, rows, side), jnp.bfloat16),
+        pltpu.VMEM((nz, piece, side), jnp.float32),
+        pltpu.VMEM((nz - 1, piece, side), jnp.float32),
+        pltpu.VMEM((nz, piece, side), jnp.float32),
+        pltpu.VMEM((side, side), jnp.bfloat16),
+        pltpu.SemaphoreType.DMA((6,)),
+        pltpu.SemaphoreType.DMA((6,)),
+    ]
+
+
+def all_sum(grads, grid, scale):
+    nx, ny, nz = grid
+
+    def kernel(grads_ref, out_ref, *scratch):
+        barrier = pltpu.get_barrier_semaphore()
+        greet_sum_peers(grid, barrier)
+        pl.semaphore_wait(barrier, 1 + (nx * ny - 1) + (nz - 1))
+        sum_body(grid, scale, grads_ref, out_ref, *scratch)
+
+    return pl.pallas_call(
+        kernel,
+        out_shape=jax.ShapeDtypeStruct(grads.shape, jnp.bfloat16),
+        in_specs=[pl.BlockSpec(memory_space=pltpu.VMEM)],
+        out_specs=pl.BlockSpec(memory_space=pltpu.VMEM),
+        scratch_shapes=sum_scratch(grid, grads.shape[2]),
+        compiler_params=pltpu.CompilerParams(collective_id=0, has_side_effects=True),
+    )(grads)
+
+
+def local(grid, history, tile_values, tile_cols, send_rows, send_count, node_ids, weights, upstream):
     levels = history.shape[0]
     batch_rows = history.shape[1]
     feature_width = history.shape[2]
@@ -96,14 +252,16 @@
             delta = (1.0 - RESTART) * spread_back(tile_values, tile_cols, back_rows, batch_rows)
             grad_rows = (delta * silu_slope(preact_all[level - 1])).astype(jnp.bfloat16)
     stacked = jnp.stack(grads)
-    stacked = lax.psum(stacked, ("dom", "rep"))
     nodes_all = batch_rows * lax.axis_size("dom") * lax.axis_size("rep")
-    return (jnp.stack(written), stacked * (1.0 / math.sqrt(nodes_all)))
+    total = all_sum(stacked, grid, 1.0 / math.sqrt(nodes_all))
+    return (jnp.stack(written), total.astype(jnp.float32))
 
 
 def solution(mesh):
+    dom, rep = mesh.shape["dom"], mesh.shape["rep"]
+    grid = (dom // RING, rep // 2, RING)
     return jax.shard_map(
-        local,
+        functools.partial(local, grid),
         mesh=mesh,
         in_specs=(
             P(None, ("dom", "rep"), None),

time: 561 us -> 137 us (0.24)
  waiting for transfers between devices: 468 us -> 20.3 us
  Pallas kernels: 0 us -> 37.3 us
  between operations: 14.3 us -> 0.94 us
    psum x1 -> x0, waiting for transfers between devices: 447 us -> none  [local(): stacked = lax.psum(stacked, ('dom', 'rep'))]
    pallas_call x0 -> x1, Pallas kernels: none -> 37.3 us  [all_sum(): pl.pallas_call(kernel, out_shape=jax.ShapeDtypeStruct(grads.shape, jnp.bf...]
  transfers between devices with their start and end apart: 3 -> 2, of which waited for: 3 -> 2; matrix products, arithmetic and copies ran while one was open for 4% -> 12% of each run, Pallas kernels for 0% -> 0%
where the time goes in v1:
time: 137 us; the launch traced here: 136 us
  Pallas kernels  37.3 us (27%)
  starting transfers between devices  27 us (20%)
  local copies, waits for them, and re-layouts  25.6 us (19%)
  waiting for transfers between devices  20.3 us (15%)
  matrix products  16.1 us (12%)
  other arithmetic  8.99 us (7%)
    pallas_call x1, Pallas kernels, all_sum(): pl.pallas_call(kernel, out_shape=jax.ShapeDtypeStruct(grads.shape, jnp.bf...  37.3 us
    all_to_all x2, starting transfers between devices, local(): lax.all_to_all(outgoing(history[level], send_rows, send_count), 'dom', sp...  27 us
    all_to_all x2, waiting for transfers between devices, local(): lax.all_to_all(outgoing(history[level], send_rows, send_count), 'dom', sp...  20.3 us
    scatter x1, local copies, waits for them, and re-layouts, local(): jnp.zeros((batch_rows, feature_width), jnp.bfloat16).at[node_rows]  6.12 us
    dot_general x2, matrix products, aggregate(): jnp.einsum('rtij,rtjf->rif', tiles, picked, preferred_element_type=jnp.fl...  6.04 us
    dot_general x1, matrix products, spread_back(): jnp.einsum('rtc,rtjf->cjf', owners, pieces, precision=lax.Precision.HIGHEST)  5.56 us
    gather x2, local copies, waits for them, and re-layouts, aggregate(): picked = jnp.take(blocks, tile_cols, axis=0)  5.54 us
    unnamed x25, local copies, waits for them, and re-layouts  4.08 us
  transfers between devices with their start and end apart: 2, of which 2 were waited for; matrix products, arithmetic and copies ran while one was open for 12% of the time, Pallas kernels for 0%

profile of v1, /device:TPU:1, one launch (start us, length us, event | category | flops | bytes accessed | tf_op | source)
XLA Modules:
  0.0 136.2 jit_solution(15615322717320186329)
XLA Ops:
  0.6 0.7 compare_and_fusion.1
  1.3 0.7 compare_select_fusion.2
  2.1 0.7 iota_compare_fusion.1
  3.1 1.3 slice_bitcast_fusion
  4.3 2.0 %gather_fusion.3 = bf16[512,256]{1,0:T(8,128)(2,1)S(1)} fusion(bf16[1024,256]{1,0:T(8,128)(2,1)S(1)} %get-tuple-element.4, s32[1024]{0:T(1024)S(1)} %pad_clamp_fusion.1), kind=kCustom, calls=%fused_computation.2.clone | custom fusion | bytes 526336 | tf_op jit(solution)/shard_map/jit(_take)/gather | solution.py:25
  6.3 2.0 %gather_fusion.1 = bf16[512,256]{1,0:T(8,128)(2,1)S(1)} fusion(bf16[1024,256]{1,0:T(8,128)(2,1)S(1)} %get-tuple-element.5, s32[1024]{0:T(1024)S(1)} %pad_clamp_fusion.1), kind=kCustom, calls=%fused_computation.clone | custom fusion | bytes 526336 | tf_op jit(solution)/shard_map/jit(_take)/gather | solution.py:25
  8.3 1.0 fusion.39
  9.3 19.1 %all-to-all-start = ((bf16[64,8,256]{2,1,0:T(8,128)(2,1)}), bf16[64,8,256]{2,1,0:T(8,128)(2,1)S(1)}, u32[]{:S(2)}, u32[]{:S(2)}) async-start(bf16[64,8,256]{2,1,0:T(8,128)(2,1)} %get-tuple-element.7), calls=%async_computation | async-start | bytes 524288 | tf_op jit(solution)/shard_map/all_to_all | solution.py:208
  28.5 3.9 %gather_fusion = bf16[1024,256]{1,0:T(8,128)(2,1)S(1)} fusion(bf16[1024,256]{1,0:T(8,128)(2,1)S(1)} %get-tuple-element.5, s32[1024]{0:T(1024)S(1)} %broadcast_clamp_fusion), kind=kCustom, calls=%fused_computation.4 | custom fusion | bytes 1052672 | tf_op jit(solution)/shard_map/jit(_take)/gather | solution.py:206
  32.5 2.9 %copy.20 = bf16[8,8,128,128]{2,1,0,3:T(8,128)(2,1)} copy(bf16[8,8,128,128]{3,2,1,0:T(8,128)(2,1)S(1)} %copy-done) | data formatting | bytes 4194304 | tf_op args[1]
  35.6 11.8 %all-to-all-done = bf16[64,8,256]{2,1,0:T(8,128)(2,1)S(1)} async-done(((bf16[64,8,256]{2,1,0:T(8,128)(2,1)}), bf16[64,8,256]{2,1,0:T(8,128)(2,1)S(1)}, u32[]{:S(2)}, u32[]{:S(2)}) %all-to-all-start) | async-done | bytes 262176 | tf_op jit(solution)/shard_map/all_to_all | solution.py:208
  47.5 7.9 %all-to-all-start.1 = ((bf16[64,8,256]{2,1,0:T(8,128)(2,1)}), bf16[64,8,256]{2,1,0:T(8,128)(2,1)}, u32[]{:S(2)}, u32[]{:S(2)}) async-start(bf16[64,8,256]{2,1,0:T(8,128)(2,1)} %get-tuple-element.6), calls=%async_computation.1 | async-start | bytes 524288 | tf_op jit(solution)/shard_map/all_to_all | solution.py:208
  55.3 1.0 pad_maximum_fusion
  56.4 2.8 %gather_fusion.2 = bf16[64,128,256]{2,1,0:T(8,128)(2,1)} fusion(bf16[12,128,256]{2,1,0:T(8,128)(2,1)S(1)} %bitcast.108, s32[1024]{0:T(1024)S(1)} %pad_clamp_fusion), kind=kCustom, calls=%fused_computation.1.clone | custom fusion | bytes 8388864 | tf_op jit(solution)/shard_map/jit(_take)/gather | solution.py:34
  59.1 3.0 %fusion.38 = (bf16[8,128,256]{2,1,0:T(8,128)(2,1)S(1)}, f32[8,256,128]{1,2,0:T(8,128)S(1)}) fusion(bf16[8,128,256]{2,1,0:T(8,128)(2,1)S(1)} %bitcast.110, pred[8,128]{1,0:T(8,128)(4,1)S(1)} %compare_and_fusion.2, bf16[8,8,128,128]{3,2,1,0:T(8,128)(2,1)S(1)} %copy-done.1, bf16[8,8,128,256]{3,2,1,0:T(8,128)(2,1)} %bitcast.113, ...), kind=kOutput, calls=%fused_computation.42 | convolution fusion | flops 540540928 | bytes 8389696 | tf_op jit(solution)/shard_map/rtij,rtjf->rif/dot_general | solution.py:35
  62.4 0.8 copy-done.5
  63.2 1.6 %multiply_convert_fusion.1 = (bf16[1024,256]{1,0:T(8,128)(2,1)}, f32[1024,256]{1,0:T(8,128)}) fusion(bf16[1024,256]{1,0:T(8,128)(2,1)S(1)} %bitcast.122, bf16[2,256,256]{2,1,0:T(8,128)(2,1)S(1)} %copy-done.10, bf16[1024,256]{1,0:T(8,128)(2,1)S(1)} %fusion.35), kind=kOutput, calls=%fused_computation.44 | convolution fusion | flops 136577024 | bytes 2752512 | tf_op jit(solution)/shard_map/dot_general | solution.py:228
  64.8 8.5 %all-to-all-done.1 = bf16[64,8,256]{2,1,0:T(8,128)(2,1)} async-done(((bf16[64,8,256]{2,1,0:T(8,128)(2,1)}), bf16[64,8,256]{2,1,0:T(8,128)(2,1)}, u32[]{:S(2)}, u32[]{:S(2)}) %all-to-all-start.1) | async-done | bytes 262176 | tf_op jit(solution)/shard_map/all_to_all | solution.py:208
  73.3 1.2 pad_maximum_fusion.1
  74.5 2.8 %gather_fusion.4 = bf16[64,128,256]{2,1,0:T(8,128)(2,1)} fusion(bf16[12,128,256]{2,1,0:T(8,128)(2,1)S(1)} %bitcast.109, s32[1024]{0:T(1024)S(1)} %pad_clamp_fusion), kind=kCustom, calls=%fused_computation.3.clone | custom fusion | bytes 8388864 | tf_op jit(solution)/shard_map/jit(_take)/gather | solution.py:34
  77.3 3.0 %fusion.37 = (bf16[8,128,256]{2,1,0:T(8,128)(2,1)S(1)}, f32[8,256,128]{1,2,0:T(8,128)S(1)}) fusion(bf16[8,128,256]{2,1,0:T(8,128)(2,1)S(1)} %bitcast.111, pred[8,128]{1,0:T(8,128)(4,1)S(1)} %compare_and_fusion.2, bf16[8,8,128,128]{3,2,1,0:T(8,128)(2,1)S(1)} %copy-done.1, bf16[8,8,128,256]{3,2,1,0:T(8,128)(2,1)} %bitcast.112, ...), kind=kOutput, calls=%fused_computation.40 | convolution fusion | flops 540540928 | bytes 8389696 | tf_op jit(solution)/shard_map/rtij,rtjf->rif/dot_general | solution.py:35
  80.6 0.7 multiply_convert_fusion
  81.3 0.3 fusion.32
  81.6 0.3 fusion.31
  82.0 6.1 %scatter_custom_fusion = bf16[1024,256]{1,0:T(8,128)(2,1)} fusion(s32[1024]{0:T(1024)S(1)} %bitcast.119, bf16[1024,256]{1,0:T(8,128)(2,1)} %get-tuple-element.10, bf16[]{:T(256)} %constant.28.clone.1), kind=kCustom, calls=%fused_computation.59 | custom fusion | bytes 524800 | tf_op jit(solution)/shard_map/scatter | solution.py:236
  88.1 1.2 fusion.54
  89.3 5.6 %fusion.28 = f32[8,128,256]{2,0,1:T(8,128)S(1)} fusion(f32[8,256,8,128]{1,2,0,3:T(8,128)S(1)} %fusion.54, s32[8,8]{1,0:T(8,128)S(1)} %copy-done.7), kind=kOutput, calls=%fused_computation.27 | convolution fusion | flops 201589248 | bytes 9437440 | tf_op jit(solution)/shard_map/rtc,rtjf->cjf/dot_general | solution.py:45
  94.9 0.3 copy.17
  95.2 0.3 fusion.36
  96.3 0.8 pad_maximum_fusion.2.grads_ref
  97.1 37.3 %shard_map.95 = bf16[2,256,256]{2,1,0:T(8,128)(2,1)} custom-call(f32[2,256,256]{2,1,0:T(8,128)} %pad_maximum_fusion.2.grads_ref), custom_call_target="tpu_custom_call" | custom-call | tf_op jit(solution)/shard_map/pallas_call | solution.py:191
  134.4 1.8 %convert_element_type.68 = f32[2,256,256]{2,1,0:T(8,128)} convert(bf16[2,256,256]{2,1,0:T(8,128)(2,1)} %shard_map.95) | non-fusion elementwise | flops 131072 | bytes 786432 | tf_op jit(solution)/shard_map/convert_element_type | solution.py:257
  (39 shorter events, 1.8 us)
Async XLA Ops:
  3.0 25.4 %copy-start.7 = (s32[8,8]{1,0:T(8,128)S(1)}, s32[8,8]{1,0:T(8,128)}, u32[]{:S(2)}) copy-start(s32[8,8]{1,0:T(8,128)} %param.14) | copy-start | bytes 772
  3.1 25.4 %copy-start.8 = (s32[1,1024]{1,0:T(1,128)S(1)}, s32[1,1024]{1,0:T(1,128)}, u32[]{:S(2)}) copy-start(s32[1,1024]{1,0:T(1,128)} %param.17) | copy-start | bytes 12292
  6.3 26.2 %copy-start = (bf16[8,8,128,128]{3,2,1,0:T(8,128)(2,1)S(1)}, bf16[8,8,128,128]{3,2,1,0:T(8,128)(2,1)}, u32[]{:S(2)}) copy-start(bf16[8,8,128,128]{3,2,1,0:T(8,128)(2,1)} %param.13) | copy-start | bytes 6291460
  9.3 38.2 %all-to-all-start = ((bf16[64,8,256]{2,1,0:T(8,128)(2,1)}), bf16[64,8,256]{2,1,0:T(8,128)(2,1)S(1)}, u32[]{:S(2)}, u32[]{:S(2)}) async-start(bf16[64,8,256]{2,1,0:T(8,128)(2,1)} %get-tuple-element.7), calls=%async_computation | async-start | bytes 524288 | tf_op jit(solution)/shard_map/all_to_all | solution.py:208
  47.5 7.9 %copy-start.4 = (bf16[64,8,256]{2,1,0:T(8,128)(2,1)}, bf16[64,8,256]{2,1,0:T(8,128)(2,1)S(1)}, u32[]{:S(2)}) copy-start(bf16[64,8,256]{2,1,0:T(8,128)(2,1)S(1)} %all-to-all-done) | copy-start | bytes 786436
  47.5 25.9 %all-to-all-start.1 = ((bf16[64,8,256]{2,1,0:T(8,128)(2,1)}), bf16[64,8,256]{2,1,0:T(8,128)(2,1)}, u32[]{:S(2)}, u32[]{:S(2)}) async-start(bf16[64,8,256]{2,1,0:T(8,128)(2,1)} %get-tuple-element.6), calls=%async_computation.1 | async-start | bytes 524288 | tf_op jit(solution)/shard_map/all_to_all | solution.py:208
  56.3 2.8 %copy-start.1 = (bf16[8,8,128,128]{3,2,1,0:T(8,128)(2,1)S(1)}, bf16[8,8,128,128]{3,2,1,0:T(8,128)(2,1)}, u32[]{:S(2)}) copy-start(bf16[8,8,128,128]{3,2,1,0:T(8,128)(2,1)} %param.13) | copy-start | bytes 6291460
  59.1 4.1 %copy-start.10 = (bf16[2,256,256]{2,1,0:T(8,128)(2,1)S(1)}, bf16[2,256,256]{2,1,0:T(8,128)(2,1)}, u32[]{:S(2)}) copy-start(bf16[2,256,256]{2,1,0:T(8,128)(2,1)} %param.18) | copy-start | bytes 786436
  62.4 0.8 copy-start.5
  77.3 3.3 %copy-start.9 = (bf16[1024,256]{1,0:T(8,128)(2,1)S(1)}, bf16[1024,256]{1,0:T(8,128)(2,1)}, u32[]{:S(2)}) copy-start(bf16[1024,256]{1,0:T(8,128)(2,1)} %param.19) | copy-start | bytes 1572868
  77.3 3.3 %copy-start.11 = (bf16[2,256,256]{2,1,0:T(8,128)(2,1)S(1)}, bf16[2,256,256]{2,1,0:T(8,128)(2,1)}, u32[]{:S(2)}) copy-start(bf16[2,256,256]{2,1,0:T(8,128)(2,1)} %param.18) | copy-start | bytes 786436
  80.6 7.5 %copy-start.2 = (bf16[8,8,128,128]{2,1,0,3:T(8,128)(2,1)S(1)}, bf16[8,8,128,128]{2,1,0,3:T(8,128)(2,1)}, u32[]{:S(2)}) copy-start(bf16[8,8,128,128]{2,1,0,3:T(8,128)(2,1)} %copy.20) | copy-start | bytes 6291460
  89.3 5.9 %copy-start.3 = (f32[1024,256]{1,0:T(8,128)S(1)}, f32[1024,256]{1,0:T(8,128)}, u32[]{:S(2)}) copy-start(f32[1024,256]{1,0:T(8,128)} %get-tuple-element.11) | copy-start | bytes 3145732
  94.9 1.1 copy-start.6

commit v2 on v1

--- a/solution.py
+++ b/solution.py
@@ -19,31 +19,6 @@
 def silu_slope(preact):
     sigma = jax.nn.sigmoid(preact)
     return sigma * (1.0 + preact * (1.0 - sigma))
-
-
-def outgoing(layer_table, send_rows, send_count):
-    picked = jnp.take(layer_table, send_rows[0], axis=0)
-    slot_index = lax.broadcasted_iota(jnp.int32, send_rows.shape[1:], 1)
-    live_mask = slot_index < send_count[0][:, None]
-    return jnp.where(live_mask[:, :, None], picked, jnp.zeros_like(picked))
-
-
-def aggregate(tiles, tile_cols, node_table):
-    tile_size = tiles.shape[2]
-    blocks = node_table.reshape(-1, tile_size, node_table.shape[1])
-    picked = jnp.take(blocks, tile_cols, axis=0)
-    summed = jnp.einsum("rtij,rtjf->rif", tiles, picked, preferred_element_type=jnp.float32)
-    return summed.reshape(-1, node_table.shape[1])
-
-
-def spread_back(tiles, tile_cols, back_rows, batch_rows):
-    tile_size = tiles.shape[2]
-    blocks = back_rows.reshape(-1, tile_size, back_rows.shape[1])
-    pieces = jnp.einsum("rtij,rif->rtjf", tiles, blocks, preferred_element_type=jnp.float32)
-    targets = lax.broadcasted_iota(jnp.int32, (1, 1, batch_rows // tile_size), 2)
-    owners = (tile_cols[:, :, None] == targets).astype(jnp.float32)
-    placed = jnp.einsum("rtc,rtjf->cjf", owners, pieces, precision=lax.Precision.HIGHEST)
-    return placed.reshape(batch_rows, back_rows.shape[1])
 
 
 MESH = pl.DeviceIdType.MESH
@@ -179,82 +154,291 @@
     ]
 
 
-def all_sum(grads, grid, scale):
-    nx, ny, nz = grid
-
-    def kernel(grads_ref, out_ref, *scratch):
-        barrier = pltpu.get_barrier_semaphore()
-        greet_sum_peers(grid, barrier)
-        pl.semaphore_wait(barrier, 1 + (nx * ny - 1) + (nz - 1))
-        sum_body(grid, scale, grads_ref, out_ref, *scratch)
-
-    return pl.pallas_call(
-        kernel,
-        out_shape=jax.ShapeDtypeStruct(grads.shape, jnp.bfloat16),
-        in_specs=[pl.BlockSpec(memory_space=pltpu.VMEM)],
-        out_specs=pl.BlockSpec(memory_space=pltpu.VMEM),
-        scratch_shapes=sum_scratch(grid, grads.shape[2]),
-        compiler_params=pltpu.CompilerParams(collective_id=0, has_side_effects=True),
-    )(grads)
+def dom_peer(step):
+    other = (lax.axis_index("dom") + step) % lax.axis_size("dom")
+    return (other, lax.axis_index("rep")), other
+
+
+def greet_halo_peers(barrier):
+    def signal(step, carry):
+        pl.semaphore_signal(barrier, inc=1, device_id=dom_peer(step)[0], device_id_type=MESH)
+        return carry
+
+    lax.fori_loop(1, lax.axis_size("dom"), signal, 0)
+
+
+def dot(a, b):
+    return jnp.dot(a, b, preferred_element_type=jnp.float32)
+
+
+def dot_t(a, b):
+    return lax.dot_general(a, b, (((0,), (0,)), ((), ())), preferred_element_type=jnp.float32)
+
+
+def iota(shape, axis):
+    return lax.broadcasted_iota(jnp.int32, shape, axis)
+
+
+def column(row):
+    n = row.shape[1]
+    picked = jnp.where(iota((n, n), 0) == iota((n, n), 1), jnp.broadcast_to(row, (n, n)), 0)
+    return jnp.sum(picked, axis=1, keepdims=True)
+
+
+def step_kernel(
+    grid,
+    history,
+    tiles_hbm,
+    cols,
+    send_rows,
+    send_count,
+    node_ids,
+    weights,
+    upstream_hbm,
+    written,
+    total_out,
+    hist,
+    tiles,
+    upstream,
+    adj,
+    adj_back,
+    picker,
+    scatter,
+    h_start,
+    hidden,
+    partial,
+    mixed,
+    slope,
+    back,
+    send_buf,
+    halo_got,
+    halo,
+    grads,
+    local_sems,
+    halo_send,
+    halo_recv,
+    *sum_refs,
+):
+    nx, ny, nz = grid
+    bf16, f32 = jnp.bfloat16, jnp.float32
+    batch, width = hist.shape[1], hist.shape[2]
+    half = width // 2
+    tile = tiles.shape[1]
+    blocks, per_row = cols.shape
+    batch_blocks = batch // tile
+    all_blocks = adj.shape[1] // tile
+    owners, cap = send_rows.shape
+    chunk = min(256, batch)
+    chunks = batch // chunk
+    me = lax.axis_index("dom")
+
+    loads = [
+        pltpu.make_async_copy(history.at[0], hist.at[0], local_sems.at[0]),
+        pltpu.make_async_copy(history.at[1], hist.at[1], local_sems.at[1]),
+        pltpu.make_async_copy(tiles_hbm, tiles.at[pl.ds(0, blocks * per_row)], local_sems.at[2]),
+        pltpu.make_async_copy(upstream_hbm, upstream, local_sems.at[3]),
+    ]
+    for load in loads:
+        load.start()
+
+    barrier = pltpu.get_barrier_semaphore()
+    greet_halo_peers(barrier)
+    greet_sum_peers(grid, barrier)
+
+    slots = owners * cap
+    slot = iota((slots, 1), 0)
+    peer = (me + slot // cap) % owners
+    turn = (peer == iota((slots, owners), 1)).astype(f32)
+    listed = lax.dot_general(
+        turn, send_rows[...].astype(f32), (((1,), (0,)), ((), ())), precision=lax.Precision.HIGHEST, preferred_element_type=f32
+    )
+    listed = jnp.sum(jnp.where(iota((slots, cap), 1) == slot % cap, listed, 0.0), axis=1, keepdims=True)
+    count = jnp.sum(turn * send_count[...].astype(f32), axis=1, keepdims=True)
+    wanted = jnp.where((slot % cap).astype(f32) < count, listed, -1.0)
+    picker[...] = jnp.where(wanted == iota((slots, batch), 1).astype(f32), 1.0, 0.0).astype(bf16)
+
+    group = max(1, 128 // cap)
+
+    def halo_copy(level, step):
+        target, other = dom_peer(step)
+        return pltpu.make_async_remote_copy(
+            src_ref=send_buf.at[level, step],
+            dst_ref=halo_got.at[level, me],
+            send_sem=halo_send.at[level],
+            recv_sem=halo_recv.at[level],
+            device_id=target,
+            device_id_type=MESH,
+        )
+
+    def fill(level, part):
+        start = pl.multiple_of(part * group * cap, group * cap)
+        rows = dot(picker[pl.ds(start, group * cap), :], hist[level])
+        low = rows[:, :half].reshape(group, cap, half)
+        high = rows[:, half:].reshape(group, cap, half)
+        send_buf[level, pl.ds(part * group, group)] = jnp.concatenate([low, high], axis=1).astype(bf16)
+
+    def post(level, part):
+        def go(step, carry):
+            halo_copy(level, step).start()
+            return carry
+
+        lax.fori_loop(jnp.maximum(part * group, 1), (part + 1) * group, go, 0)
+
+    for level in range(2):
+        loads[level].wait()
+        if level == 0:
+            fill(0, 0)
+            pl.semaphore_wait(barrier, (owners - 1) + 1 + (nx * ny - 1) + (nz - 1))
+            post(0, 0)
+
+        def emit(part, carry):
+            fill(level, part)
+            post(level, part)
+            return carry
+
+        lax.fori_loop(1 - level, owners // group, emit, 0)
+        halo_got[level, me] = send_buf[level, 0]
+
+    scatter[...] = jnp.where(iota((batch, batch), 0) == node_ids[...], 1.0, 0.0).astype(bf16)
+    for part in range(batch // tile):
+        ids = column(node_ids[:, part * tile : (part + 1) * tile])
+        gather = jnp.where(ids == iota((tile, batch), 1), 1.0, 0.0).astype(bf16)
+        h_start[part * tile : (part + 1) * tile] = dot(gather, hist[0]).astype(bf16)
+
+    loads[2].wait()
+    tiles[blocks * per_row] = jnp.zeros((tile, tile), bf16)
+
+    def arrange(row, carry):
+        down = pl.multiple_of(row * tile, tile)
+        for block in range(all_blocks):
+            index = blocks * per_row
+            for t in range(per_row):
+                index = jnp.where(cols[row, t] == block, row * per_row + t, index)
+            values = tiles[index]
+            adj[pl.ds(down, tile), block * tile : (block + 1) * tile] = values
+            if block < batch_blocks:
+                adj_back[block * tile : (block + 1) * tile, pl.ds(down, tile)] = values.astype(f32).T.astype(bf16)
+        return carry
+
+    lax.fori_loop(0, blocks, arrange, 0)
+
+    def over_chunks(body):
+        def run(part, carry):
+            body(pl.ds(pl.multiple_of(part * chunk, chunk), chunk))
+            return carry
+
+        lax.fori_loop(0, chunks, run, 0)
+
+    def batch_part(source):
+        def body(rows):
+            partial[rows, :] = dot(adj[rows, :batch], source[...])
+
+        over_chunks(body)
+
+    def receive(level):
+        span_wait(send_buf.at[level, pl.ds(0, owners - 1)], halo_recv.at[level])
+        got = halo_got[level].astype(f32)
+        low = got[:, :cap].reshape(slots, half)
+        high = got[:, cap:].reshape(slots, half)
+        halo[...] = jnp.concatenate([low, high], axis=1).astype(bf16)
+
+    def preact(level, rows):
+        summed = partial[rows, :] + dot(adj[rows, batch:], halo[...])
+        mixed_rows = ((1.0 - RESTART) * summed + RESTART * h_start[rows, :].astype(f32)).astype(bf16)
+        mixed[level, rows, :] = mixed_rows
+        beta = layer_beta(level)
+        return (1.0 - beta) * mixed_rows.astype(f32) + beta * dot(mixed_rows, weights[level])
+
+    batch_part(h_start)
+    receive(0)
+
+    def first_layer(rows):
+        z = preact(0, rows)
+        sigma = jax.nn.sigmoid(z)
+        hidden[rows, :] = (z * sigma).astype(bf16)
+        slope[rows, :] = sigma * (1.0 + z * (1.0 - sigma))
+
+    over_chunks(first_layer)
+    batch_part(hidden)
+
+    def write_back(rows):
+        written[0, rows, :] = dot(scatter[rows, :], hidden[...]).astype(bf16)
+
+    over_chunks(write_back)
+    loads[3].wait()
+    receive(1)
+    beta_last = layer_beta(1)
+
+    def last_layer(rows):
+        z = preact(1, rows)
+        grad = (upstream[rows, :].astype(f32) * silu_slope(z)).astype(bf16)
+        upstream[rows, :] = grad
+        turned = lax.dot_general(grad, weights[1], (((1,), (1,)), ((), ())), preferred_element_type=f32)
+        back[rows, :] = ((1.0 - beta_last) * grad.astype(f32) + beta_last * turned).astype(bf16)
+
+    over_chunks(last_layer)
+    grads[1] = beta_last * dot_t(mixed[1], upstream[...])
+
+    def first_grad(rows):
+        total = dot(adj_back[rows, :], back[...])
+        hidden[rows, :] = ((1.0 - RESTART) * total * slope[rows, :]).astype(bf16)
+
+    over_chunks(first_grad)
+    grads[0] = layer_beta(0) * dot_t(mixed[0], hidden[...])
+    nodes_all = batch * owners * lax.axis_size("rep")
+    sum_body(grid, 1.0 / math.sqrt(nodes_all), grads, total_out, *sum_refs)
+    for level in range(2):
+        span_wait(send_buf.at[level, pl.ds(0, owners - 1)], halo_send.at[level])
 
 
 def local(grid, history, tile_values, tile_cols, send_rows, send_count, node_ids, weights, upstream):
-    levels = history.shape[0]
-    batch_rows = history.shape[1]
-    feature_width = history.shape[2]
-    node_rows = node_ids[0]
-    h_start = jnp.take(history[0], node_rows, axis=0)
-    halos = [
-        lax.all_to_all(
-            outgoing(history[level], send_rows, send_count),
-            "dom",
-            split_axis=0,
-            concat_axis=0,
-            tiled=True,
-        ).reshape(-1, feature_width)
-        for level in range(levels)
-    ]
-    current = h_start
-    mixed_all = []
-    preact_all = []
-    written = []
-    for level in range(levels):
-        node_table = jnp.concatenate([current, halos[level]], axis=0)
-        summed = aggregate(tile_values, tile_cols, node_table)
-        mixed_rows = ((1.0 - RESTART) * summed + RESTART * h_start.astype(jnp.float32)).astype(
-            jnp.bfloat16
-        )
-        beta_value = layer_beta(level)
-        preact = (1.0 - beta_value) * mixed_rows.astype(jnp.float32) + beta_value * jnp.dot(
-            mixed_rows, weights[level], preferred_element_type=jnp.float32
-        )
-        current = jax.nn.silu(preact).astype(jnp.bfloat16)
-        mixed_all.append(mixed_rows)
-        preact_all.append(preact)
-        if level + 1 < levels:
-            written.append(
-                jnp.zeros((batch_rows, feature_width), jnp.bfloat16).at[node_rows].set(current)
-            )
-    grads = [None] * levels
-    grad_rows = (upstream.astype(jnp.float32) * silu_slope(preact_all[-1])).astype(jnp.bfloat16)
-    for level in reversed(range(levels)):
-        beta_value = layer_beta(level)
-        local_grad = beta_value * jnp.dot(
-            mixed_all[level].T, grad_rows, preferred_element_type=jnp.float32
-        )
-        grads[level] = local_grad
-        if level > 0:
-            back_rows = (
-                (1.0 - beta_value) * grad_rows.astype(jnp.float32)
-                + beta_value
-                * jnp.dot(grad_rows, weights[level].T, preferred_element_type=jnp.float32)
-            ).astype(jnp.bfloat16)
-            delta = (1.0 - RESTART) * spread_back(tile_values, tile_cols, back_rows, batch_rows)
-            grad_rows = (delta * silu_slope(preact_all[level - 1])).astype(jnp.bfloat16)
-    stacked = jnp.stack(grads)
-    nodes_all = batch_rows * lax.axis_size("dom") * lax.axis_size("rep")
-    total = all_sum(stacked, grid, 1.0 / math.sqrt(nodes_all))
-    return (jnp.stack(written), total.astype(jnp.float32))
+    levels, batch, width = history.shape
+    blocks, per_row, tile, _ = tile_values.shape
+    _, owners, cap = send_rows.shape
+    slots = owners * cap
+    bf16, f32 = jnp.bfloat16, jnp.float32
+    vmem = pl.BlockSpec(memory_space=pltpu.VMEM)
+    anywhere = pl.BlockSpec(memory_space=pl.ANY)
+    written, total = pl.pallas_call(
+        functools.partial(step_kernel, grid),
+        out_shape=(jax.ShapeDtypeStruct((1, batch, width), bf16), jax.ShapeDtypeStruct((levels, width, width), bf16)),
+        in_specs=[anywhere, anywhere, pl.BlockSpec(memory_space=pltpu.SMEM), vmem, vmem, vmem, vmem, anywhere],
+        out_specs=(vmem, vmem),
+        scratch_shapes=[
+            pltpu.VMEM((levels, batch, width), bf16),
+            pltpu.VMEM((blocks * per_row + 1, tile, tile), bf16),
+            pltpu.VMEM((batch, width), bf16),
+            pltpu.VMEM((batch, batch + slots), bf16),
+            pltpu.VMEM((batch, batch), bf16),
+            pltpu.VMEM((slots, batch), bf16),
+            pltpu.VMEM((batch, batch), bf16),
+            pltpu.VMEM((batch, width), bf16),
+            pltpu.VMEM((batch, width), bf16),
+            pltpu.VMEM((batch, width), f32),
+            pltpu.VMEM((levels, batch, width), bf16),
+            pltpu.VMEM((batch, width), f32),
+            pltpu.VMEM((batch, width), bf16),
+            pltpu.VMEM((levels, owners, 2 * cap, width // 2), bf16),
+            pltpu.VMEM((levels, owners, 2 * cap, width // 2), bf16),
+            pltpu.VMEM((slots, width), bf16),
+            pltpu.VMEM((levels, width, width), f32),
+            pltpu.SemaphoreType.DMA((4,)),
+            pltpu.SemaphoreType.DMA((levels,)),
+            pltpu.SemaphoreType.DMA((levels,)),
+        ]
+        + sum_scratch(grid, width),
+        compiler_params=pltpu.CompilerParams(collective_id=0, has_side_effects=True, vmem_limit_bytes=56 * 2**20),
+    )(
+        history,
+        tile_values.reshape(blocks * per_row, tile, tile),
+        tile_cols,
+        send_rows[0],
+        send_count,
+        node_ids,
+        weights,
+        upstream,
+    )
+    return written, total.astype(f32)
 
 
 def solution(mesh):

time: 137 us -> 83.2 us (0.61)
  Pallas kernels: 37.3 us -> 77.3 us
  starting transfers between devices: 27 us -> 0 us
  local copies, waits for them, and re-layouts: 25.6 us -> 3.25 us
  waiting for transfers between devices: 20.3 us -> 0 us
  matrix products: 16.1 us -> 0 us
  other arithmetic: 8.99 us -> 1.78 us
    pallas_call x1, Pallas kernels: 37.3 us -> 77.3 us  [local(): pl.pallas_call(functools.partial(step_kernel, grid), out_shape=(jax.Shape...]
    all_to_all x2 -> x0, starting transfers between devices: 27 us -> none  [local(): lax.all_to_all(outgoing(history[level], send_rows, send_count), 'dom', sp...]
    all_to_all x2 -> x0, waiting for transfers between devices: 20.3 us -> none  [local(): lax.all_to_all(outgoing(history[level], send_rows, send_count), 'dom', sp...]
    dot_general x9 -> x0, matrix products: 16.1 us -> none  [the longest x2 6.04 us: aggregate(): jnp.einsum('rtij,rtjf->rif', tiles, picked, preferred_element_type=jnp.fl...]
    gather x5 -> x0, local copies, waits for them, and re-layouts: 13.4 us -> none  [the longest x2 5.54 us: aggregate(): picked = jnp.take(blocks, tile_cols, axis=0)]
    scatter x1 -> x0, local copies, waits for them, and re-layouts: 6.12 us -> none  [local(): jnp.zeros((batch_rows, feature_width), jnp.bfloat16).at[node_rows]]
    concatenate x2 -> x0, other arithmetic: 2.18 us -> none  [local(): node_table = jnp.concatenate([current, halos[level]], axis=0)]
    select_n x5 -> x0, other arithmetic: 1.9 us -> none  [the longest x1 1 us: outgoing(): return jnp.where(live_mask[:, :, None], picked, jnp.zeros_like(picked))]
  transfers between devices with their start and end apart: 2 -> 0, of which waited for: 2 -> 0; matrix products, arithmetic and copies ran while one was open for 12% -> 0% of each run, Pallas kernels for 0% -> 0%
where the time goes in v2:
time: 83.2 us; the launch traced here: 83 us
  Pallas kernels  77.3 us (93%)
  local copies, waits for them, and re-layouts  3.25 us (4%)
  other arithmetic  1.78 us (2%)
    pallas_call x1, Pallas kernels, local(): pl.pallas_call(functools.partial(step_kernel, grid), out_shape=(jax.Shape...  77.3 us
    unnamed x2, local copies, waits for them, and re-layouts  3.25 us
    convert_element_type x1, other arithmetic, local(): return (written, total.astype(f32))  1.78 us

profile of v2, /device:TPU:1, one launch (start us, length us, event | category | flops | bytes accessed | tf_op | source)
XLA Modules:
  0.0 83.0 jit_solution(6396895650253702951)
XLA Ops:
  0.6 1.4 %copy.10 = s32[1,64,8]{2,1,0:T(8,128)} copy(s32[1,64,8]{1,2,0:T(8,128)} %param.11) | data formatting | bytes 4096 | tf_op args[3]
  2.0 77.3 %shard_map.95 = (bf16[1,1024,256]{2,1,0:T(8,128)(2,1)}, bf16[2,256,256]{2,1,0:T(8,128)(2,1)}) custom-call(bf16[2,1024,256]{2,1,0:T(8,128)(2,1)} %history.1, bf16[64,128,128]{2,1,0:T(8,128)(2,1)} %bitcast.2, s32[8,8]{1,0:T(8,128)} %cols.1, s32[64,8]{1,0:T(8,128)} %bitcast.3, s32[1,64]{1,0:T(1,128)} %send_count.1, s32[1,1024]{1,0:T(1,128)} %node_ids.1, ...), custom_call_target="tpu_custom_call" | custom-call | tf_op jit(solution)/shard_map/pallas_call | solution.py:402
  79.3 1.8 %convert_element_type.3 = f32[2,256,256]{2,1,0:T(8,128)} convert(bf16[2,256,256]{2,1,0:T(8,128)(2,1)} %get-tuple-element.5) | non-fusion elementwise | flops 131072 | bytes 786432 | tf_op jit(solution)/shard_map/convert_element_type | solution.py:441
  81.1 1.9 %copy.12 = bf16[1,1024,256]{2,1,0:T(8,128)(2,1)} copy(bf16[1,1024,256]{2,1,0:T(8,128)(2,1)} %get-tuple-element.8) | data formatting | bytes 1048576

commit v3 on v2

v3 whole, which is shorter than its diff:
```python
import functools
import math

import jax
import jax.numpy as jnp
from jax import lax
from jax.experimental import pallas as pl
from jax.experimental.pallas import tpu as pltpu
from jax.sharding import PartitionSpec as P

RESTART = 0.1
RING = 16


def layer_beta(level):
    return math.log(0.5 / (level + 1) + 1.0)


def silu_slope(preact):
    sigma = jax.nn.sigmoid(preact)
    return sigma * (1.0 + preact * (1.0 - sigma))


MESH = pl.DeviceIdType.MESH


def span_wait(ref, sem):
    pltpu.make_async_copy(ref, ref, sem).wait()


def place(grid):
    nx, ny, nz = grid
    dom, rep = lax.axis_index("dom"), lax.axis_index("rep")
    return dom // nz, dom % nz, rep // 2, rep % 2


def far_first(n, turn):
    side = (turn + 1) // 2
    return (n // 2 + side * (1 - 2 * (turn % 2)) + n) % n


def ring_peer(grid, turn):
    nx, ny, nz = grid
    x, z, y, core = place(grid)
    return (x * nz + (z + far_first(nz, turn)) % nz, y * 2 + core)


def halo_peer(grid, turn):
    nx, ny, nz = grid
    x, z, y, core = place(grid)
    return ((x + far_first(nx, turn % nx)) % nx) * nz + (z + far_first(nz, turn // nx)) % nz


def greet(grid, barrier):
    nx, ny, nz = grid
    x, z, y, core = place(grid)
    rep, reps = lax.axis_index("rep"), 2 * ny

    def signal(target):
        pl.semaphore_signal(barrier, inc=1, device_id=target, device_id_type=MESH)

    def halo(turn, carry):
        signal((halo_peer(grid, turn), rep))
        return carry

    def layer(turn, carry):
        signal(((x + turn % nx) % nx * nz + z, (rep + 1 + turn // nx) % reps))
        return carry

    lax.fori_loop(0, nx * nz - 1, halo, 0)
    lax.fori_loop(0, nx * (reps - 1), layer, 0)
    return nx * nz - 1 + nx * (reps - 1)


def link(stage, src, dst, target, send_sems, recv_sems):
    return pltpu.make_async_remote_copy(
        src_ref=src, dst_ref=dst, send_sem=send_sems.at[stage], recv_sem=recv_sems.at[stage], device_id=target, device_id_type=MESH
    )


def layer_share(grid, rows):
    nx, ny, nz = grid
    x, z, y, core = place(grid)
    reps = 2 * ny
    mine = x * reps + y * 2 + core

    def span(index):
        return pl.ds(pl.multiple_of(index * rows, rows), rows)

    def device(index):
        return (index // reps * nz + z, index % reps)

    return mine, span, device


def sum_send(grid, level, source, layer_got, ring_got, send_sems, recv_sems):
    shares, rows = layer_got.shape[0], layer_got.shape[1]
    group = shares // 2
    mine, span, device = layer_share(grid, rows)

    def send(turn, carry):
        index = level * group + (mine + turn) % group
        link(0, source.at[span(index)], layer_got.at[mine], device(index), send_sems, recv_sems).start()
        return carry

    lax.fori_loop(jnp.where(mine // group == level, 1, 0), group, send, 0)


def sum_rest(grid, scale, out, source, layer_got, ring_got, send_sems, recv_sems):
    nx, ny, nz = grid
    shares, rows = layer_got.shape[0], layer_got.shape[1]
    mine, span, device = layer_share(grid, rows)
    z = place(grid)[1]
    layer_got[mine] = source[span(mine), :]
    span_wait(layer_got.at[pl.ds(0, shares - 1)], recv_sems.at[0])
    ring_got[z] = jnp.sum(layer_got[...].astype(jnp.float32), axis=0).astype(jnp.bfloat16)

    def ring_send(turn, carry):
        link(1, ring_got.at[z], ring_got.at[z], ring_peer(grid, turn), send_sems, recv_sems).start()
        return carry

    lax.fori_loop(0, nz - 1, ring_send, 0)
    span_wait(source.at[pl.ds(0, (shares - 1) * rows)], send_sems.at[0])
    span_wait(ring_got.at[pl.ds(0, nz - 1)], recv_sems.at[1])
    total = jnp.sum(ring_got[...].astype(jnp.float32), axis=0) * scale
    source[span(mine), :] = total.astype(jnp.bfloat16)

    def share(turn, carry):
        index = (mine + 1 + (shares // 2 + ny - 1 + turn) % (shares - 1)) % shares
        link(2, source.at[span(mine)], out.at[span(mine)], device(index), send_sems, recv_sems).start()
        return carry

    lax.fori_loop(0, shares - 1, share, 0)
    own = pltpu.make_async_copy(source.at[span(mine)], out.at[span(mine)], send_sems.at[3])
    own.start()
    span_wait(ring_got.at[pl.ds(0, nz - 1)], send_sems.at[1])
    span_wait(source.at[pl.ds(0, (shares - 1) * rows)], send_sems.at[2])
    own.wait()
    span_wait(source.at[pl.ds(0, (shares - 1) * rows)], recv_sems.at[2])


def sum_scratch(grid, levels, side):
    nx, ny, nz = grid
    shares = nx * ny * 2
    rows = levels * side // shares
    return [
        pltpu.VMEM((levels * side, side), jnp.bfloat16),
        pltpu.VMEM((shares, rows, side), jnp.bfloat16),
        pltpu.VMEM((nz, rows, side), jnp.bfloat16),
        pltpu.SemaphoreType.DMA((4,)),
        pltpu.SemaphoreType.DMA((3,)),
    ]


def dot(a, b):
    return jnp.dot(a, b, preferred_element_type=jnp.float32)


def dot_t(a, b):
    return lax.dot_general(a, b, (((0,), (0,)), ((), ())), preferred_element_type=jnp.float32)


def iota(shape, axis):
    return lax.broadcasted_iota(jnp.int32, shape, axis)


def column(row):
    n = row.shape[1]
    picked = jnp.where(iota((n, n), 0) == iota((n, n), 1), jnp.broadcast_to(row, (n, n)), 0)
    return jnp.sum(picked, axis=1, keepdims=True)


def step_kernel(
    grid,
    history,
    tiles_hbm,
    cols_hbm,
    send_rows_hbm,
    send_count_hbm,
    node_ids_hbm,
    weights_hbm,
    upstream_hbm,
    written,
    total_out,
    cols,
    send_rows,
    send_count,
    node_ids,
    weights,
    written_rows,
    hist,
    tiles,
    upstream,
    adj,
    adj_back,
    picker,
    scatter,
    h_start,
    hidden,
    partial,
    mixed,
    slope,
    back,
    send_buf,
    halo_got,
    halo,
    local_sems,
    halo_send,
    halo_recv,
    *sum_refs,
):
    nx, ny, nz = grid
    bf16, f32 = jnp.bfloat16, jnp.float32
    batch, width = hist.shape[1], hist.shape[2]
    half = width // 2
    tile = tiles.shape[1]
    blocks, per_row = cols.shape
    batch_blocks = batch // tile
    all_blocks = adj.shape[1] // tile
    cap, owners = send_rows.shape
    chunk = min(256, batch)
    chunks = batch // chunk
    me = lax.axis_index("dom")

    barrier = pltpu.get_barrier_semaphore()
    loads = [
        pltpu.make_async_copy(src, dst, local_sems.at[place])
        for place, (src, dst) in enumerate(
            [
                (send_rows_hbm, send_rows),
                (send_count_hbm, send_count),
                (history.at[0], hist.at[0]),
                (history.at[1], hist.at[1]),
                (node_ids_hbm, node_ids),
                (cols_hbm, cols),
                (tiles_hbm, tiles.at[pl.ds(0, blocks * per_row)]),
                (weights_hbm, weights),
                (upstream_hbm, upstream),
            ]
        )
    ]
    for load in loads[:3]:
        load.start()
    greeted = greet(grid, barrier)
    for load in loads[3:]:
        load.start()
    for load in loads[:2]:
        load.wait()

    slots = owners * cap
    slot = iota((slots, 1), 0)
    peer = halo_peer(grid, slot // cap)
    turn = (peer == iota((slots, owners), 1)).astype(f32)
    listed = lax.dot_general(
        turn, send_rows[...].astype(f32), (((1,), (1,)), ((), ())), precision=lax.Precision.HIGHEST, preferred_element_type=f32
    )
    listed = jnp.sum(jnp.where(iota((slots, cap), 1) == slot % cap, listed, 0.0), axis=1, keepdims=True)
    count = jnp.sum(turn * send_count[...].astype(f32), axis=1, keepdims=True)
    wanted = jnp.where((slot % cap).astype(f32) < count, listed, -1.0)
    picker[...] = jnp.where(wanted == iota((slots, batch), 1).astype(f32), 1.0, 0.0).astype(bf16)

    group = max(1, 128 // cap)

    def halo_copy(level, turn):
        return pltpu.make_async_remote_copy(
            src_ref=send_buf.at[level, turn],
            dst_ref=halo_got.at[level, me],
            send_sem=halo_send.at[level],
            recv_sem=halo_recv.at[level],
            device_id=(halo_peer(grid, turn), lax.axis_index("rep")),
            device_id_type=MESH,
        )

    def fill(level, part):
        start = pl.multiple_of(part * group * cap, group * cap)
        rows = dot(picker[pl.ds(start, group * cap), :], hist[level])
        low = rows[:, :half].reshape(group, cap, half)
        high = rows[:, half:].reshape(group, cap, half)
        send_buf[level, pl.ds(part * group, group)] = jnp.concatenate([low, high], axis=1).astype(bf16)

    def post(level, part):
        def go(turn, carry):
            halo_copy(level, turn).start()
            return carry

        lax.fori_loop(part * group, jnp.minimum((part + 1) * group, owners - 1), go, 0)

    for level in range(2):
        loads[2 + level].wait()
        if level == 0:
            fill(0, 0)
            pl.semaphore_wait(barrier, greeted)
            post(0, 0)

        def emit(part, carry):
            fill(level, part)
            post(level, part)
            return carry

        lax.fori_loop(1 - level, owners // group, emit, 0)
        halo_got[level, me] = send_buf[level, owners - 1]

    loads[4].wait()
    scatter[...] = jnp.where(iota((batch, batch), 0) == node_ids[...], 1.0, 0.0).astype(bf16)
    for part in range(batch // tile):
        ids = column(node_ids[:, part * tile : (part + 1) * tile])
        gather = jnp.where(ids == iota((tile, batch), 1), 1.0, 0.0).astype(bf16)
        h_start[part * tile : (part + 1) * tile] = dot(gather, hist[0]).astype(bf16)

    loads[5].wait()
    loads[6].wait()
    tiles[blocks * per_row] = jnp.zeros((tile, tile), bf16)

    def arrange(row, carry):
        down = pl.multiple_of(row * tile, tile)
        for block in range(all_blocks):
            index = blocks * per_row
            for t in range(per_row):
                index = jnp.where(cols[row, t] == block, row * per_row + t, index)
            values = tiles[index]
            adj[pl.ds(down, tile), block * tile : (block + 1) * tile] = values
            if block < batch_blocks:
                adj_back[block * tile : (block + 1) * tile, pl.ds(down, tile)] = values.astype(f32).T.astype(bf16)
        return carry

    lax.fori_loop(0, blocks, arrange, 0)

    def over_chunks(body):
        def run(part, carry):
            body(pl.ds(pl.multiple_of(part * chunk, chunk), chunk))
            return carry

        lax.fori_loop(0, chunks, run, 0)

    def batch_part(source):
        def body(rows):
            partial[rows, :] = dot(adj[rows, :batch], source[...])

        over_chunks(body)

    def receive(level):
        span_wait(send_buf.at[level, pl.ds(0, owners - 1)], halo_recv.at[level])
        got = halo_got[level].astype(f32)
        low = got[:, :cap].reshape(slots, half)
        high = got[:, cap:].reshape(slots, half)
        halo[...] = jnp.concatenate([low, high], axis=1).astype(bf16)

    def preact(level, rows):
        summed = partial[rows, :] + dot(adj[rows, batch:], halo[...])
        mixed_rows = ((1.0 - RESTART) * summed + RESTART * h_start[rows, :].astype(f32)).astype(bf16)
        mixed[level, rows, :] = mixed_rows
        beta = layer_beta(level)
        return (1.0 - beta) * mixed_rows.astype(f32) + beta * dot(mixed_rows, weights[level])

    batch_part(h_start)
    loads[7].wait()
    receive(0)

    def first_layer(rows):
        z = preact(0, rows)
        sigma = jax.nn.sigmoid(z)
        hidden[rows, :] = (z * sigma).astype(bf16)
        slope[rows, :] = sigma * (1.0 + z * (1.0 - sigma))

    over_chunks(first_layer)
    batch_part(hidden)

    def write_back(rows):
        written_rows[rows, :] = dot(scatter[rows, :], hidden[...]).astype(bf16)

    over_chunks(write_back)
    store = pltpu.make_async_copy(written_rows, written.at[0], local_sems.at[len(loads)])
    store.start()
    loads[8].wait()
    receive(1)
    beta_last = layer_beta(1)

    def last_layer(rows):
        z = preact(1, rows)
        grad = (upstream[rows, :].astype(f32) * silu_slope(z)).astype(bf16)
        upstream[rows, :] = grad
        turned = lax.dot_general(grad, weights[1], (((1,), (1,)), ((), ())), preferred_element_type=f32)
        back[rows, :] = ((1.0 - beta_last) * grad.astype(f32) + beta_last * turned).astype(bf16)

    over_chunks(last_layer)
    source = sum_refs[0]
    source[width:, :] = (beta_last * dot_t(mixed[1], upstream[...])).astype(bf16)
    sum_send(grid, 1, *sum_refs)

    def first_grad(rows):
        total = dot(adj_back[rows, :], back[...])
        hidden[rows, :] = ((1.0 - RESTART) * total * slope[rows, :]).astype(bf16)

    over_chunks(first_grad)
    source[:width, :] = (layer_beta(0) * dot_t(mixed[0], hidden[...])).astype(bf16)
    sum_send(grid, 0, *sum_refs)
    nodes_all = batch * owners * lax.axis_size("rep")
    sum_rest(grid, 1.0 / math.sqrt(nodes_all), total_out, *sum_refs)
    store.wait()
    for level in range(2):
        span_wait(send_buf.at[level, pl.ds(0, owners - 1)], halo_send.at[level])


def local(grid, history, tile_values, tile_cols, send_rows, send_count, node_ids, weights, upstream):
    levels, batch, width = history.shape
    blocks, per_row, tile, _ = tile_values.shape
    _, owners, cap = send_rows.shape
    slots = owners * cap
    bf16, f32 = jnp.bfloat16, jnp.float32
    vmem = pl.BlockSpec(memory_space=pltpu.VMEM)
    anywhere = pl.BlockSpec(memory_space=pl.ANY)
    written, total = pl.pallas_call(
        functools.partial(step_kernel, grid),
        out_shape=(jax.ShapeDtypeStruct((1, batch, width), bf16), jax.ShapeDtypeStruct((levels * width, width), bf16)),
        in_specs=[anywhere] * 8,
        out_specs=(anywhere, anywhere),
        scratch_shapes=[
            pltpu.SMEM((blocks, per_row), jnp.int32),
            pltpu.VMEM((cap, owners), jnp.int32),
            pltpu.VMEM((1, owners), jnp.int32),
            pltpu.VMEM((1, batch), jnp.int32),
            pltpu.VMEM((levels, width, width), bf16),
            pltpu.VMEM((batch, width), bf16),
            pltpu.VMEM((levels, batch, width), bf16),
            pltpu.VMEM((blocks * per_row + 1, tile, tile), bf16),
            pltpu.VMEM((batch, width), bf16),
            pltpu.VMEM((batch, batch + slots), bf16),
            pltpu.VMEM((batch, batch), bf16),
            pltpu.VMEM((slots, batch), bf16),
            pltpu.VMEM((batch, batch), bf16),
            pltpu.VMEM((batch, width), bf16),
            pltpu.VMEM((batch, width), bf16),
            pltpu.VMEM((batch, width), f32),
            pltpu.VMEM((levels, batch, width), bf16),
            pltpu.VMEM((batch, width), f32),
            pltpu.VMEM((batch, width), bf16),
            pltpu.VMEM((levels, owners, 2 * cap, width // 2), bf16),
            pltpu.VMEM((levels, owners, 2 * cap, width // 2), bf16),
            pltpu.VMEM((slots, width), bf16),
            pltpu.SemaphoreType.DMA((10,)),
            pltpu.SemaphoreType.DMA((levels,)),
            pltpu.SemaphoreType.DMA((levels,)),
        ]
        + sum_scratch(grid, levels, width),
        compiler_params=pltpu.CompilerParams(collective_id=0, has_side_effects=True, vmem_limit_bytes=56 * 2**20),
    )(
        history,
        tile_values.reshape(blocks * per_row, tile, tile),
        tile_cols,
        send_rows[0].T,
        send_count,
        node_ids,
        weights,
        upstream,
    )

    def finish(written_ref, total_ref, written_out, total_out):
        written_out[...] = written_ref[...]
        for level in range(levels):
            total_out[level] = total_ref[level * width : (level + 1) * width].astype(f32)

    return pl.pallas_call(
        finish,
        out_shape=(jax.ShapeDtypeStruct(written.shape, bf16), jax.ShapeDtypeStruct((levels, width, width), f32)),
        in_specs=[vmem, vmem],
        out_specs=(vmem, vmem),
    )(written, total)


def solution(mesh):
    dom, rep = mesh.shape["dom"], mesh.shape["rep"]
    grid = (dom // RING, rep // 2, RING)
    return jax.shard_map(
        functools.partial(local, grid),
        mesh=mesh,
        in_specs=(
            P(None, ("dom", "rep"), None),
            P(("dom", "rep"), None, None, None),
            P(("dom", "rep"), None),
            P(("dom", "rep"), None, None),
            P(("dom", "rep"), None),
            P(("dom", "rep"), None),
            P(),
            P(("dom", "rep"), None),
        ),
        out_specs=(P(None, ("dom", "rep"), None), P()),
        check_vma=False,
    )
```

time: 83.2 us -> 72.7 us (0.87)
  Pallas kernels: 77.3 us -> 71.9 us
  local copies, waits for them, and re-layouts: 3.25 us -> 0 us
  other arithmetic: 1.78 us -> 0 us
    pallas_call x1, Pallas kernels: 77.3 us -> 69.8 us  [local(): pl.pallas_call(functools.partial(step_kernel, grid), out_shape=(jax.Shape...]
    unnamed x2 -> x0, local copies, waits for them, and re-layouts: 3.25 us -> none
    pallas_call x0 -> x1, Pallas kernels: none -> 2.11 us  [local(): pl.pallas_call(finish, out_shape=(jax.ShapeDtypeStruct(written.shape, bf1...]
    convert_element_type x1 -> x0, other arithmetic: 1.78 us -> none  [local(): return (written, total.astype(f32))]
where the time goes in v3:
time: 72.7 us; the launch traced here: 72.6 us
  Pallas kernels  71.9 us (99%)
    pallas_call x1, Pallas kernels, local(): pl.pallas_call(functools.partial(step_kernel, grid), out_shape=(jax.Shape...  69.8 us
    pallas_call x1, Pallas kernels, local(): pl.pallas_call(finish, out_shape=(jax.ShapeDtypeStruct(written.shape, bf1...  2.11 us

profile of v3, /device:TPU:1, one launch (start us, length us, event | category | flops | bytes accessed | tf_op | source)
XLA Modules:
  0.0 72.6 jit_solution(4623051352482239858)
XLA Ops:
  0.6 69.8 %shard_map.95 = (bf16[1,1024,256]{2,1,0:T(8,128)(2,1)}, bf16[512,256]{1,0:T(8,128)(2,1)}) custom-call(bf16[2,1024,256]{2,1,0:T(8,128)(2,1)} %history.1, bf16[64,128,128]{2,1,0:T(8,128)(2,1)} %bitcast.4, s32[8,8]{1,0:T(8,128)} %cols_hbm.1, s32[8,64]{1,0:T(8,128)} %bitcast.5, s32[1,64]{1,0:T(1,128)} %send_count_hbm.1, s32[1,1024]{1,0:T(1,128)} %node_ids_hbm.1, ...), custom_call_target="tpu_custom_call" | custom-call | tf_op jit(solution)/shard_map/pallas_call | solution.py:412
  70.5 2.1 %shard_map.96 = (bf16[1,1024,256]{2,1,0:T(8,128)(2,1)}, f32[2,256,256]{2,1,0:T(8,128)}) custom-call(bf16[1,1024,256]{2,1,0:T(8,128)(2,1)} %get-tuple-element.4.written_ref, bf16[512,256]{1,0:T(8,128)(2,1)} %get-tuple-element.5.total_ref), custom_call_target="tpu_custom_call" | custom-call | tf_op jit(solution)/shard_map/pallas_call | solution.py:462

commit v4 on v3

--- a/solution.py
+++ b/solution.py
@@ -67,8 +67,10 @@
         signal(((x + turn % nx) % nx * nz + z, (rep + 1 + turn // nx) % reps))
         return carry
 
-    lax.fori_loop(0, nx * nz - 1, halo, 0)
+    far = nx * nz // 2
+    lax.fori_loop(0, far, halo, 0)
     lax.fori_loop(0, nx * (reps - 1), layer, 0)
+    lax.fori_loop(far, nx * nz - 1, halo, 0)
     return nx * nz - 1 + nx * (reps - 1)
 
 
@@ -218,14 +220,14 @@
     batch_blocks = batch // tile
     all_blocks = adj.shape[1] // tile
     cap, owners = send_rows.shape
-    chunk = min(256, batch)
+    chunk = min(512, batch)
     chunks = batch // chunk
     me = lax.axis_index("dom")
 
     barrier = pltpu.get_barrier_semaphore()
     loads = [
-        pltpu.make_async_copy(src, dst, local_sems.at[place])
-        for place, (src, dst) in enumerate(
+        pltpu.make_async_copy(src, dst, local_sems.at[order])
+        for order, (src, dst) in enumerate(
             [
                 (send_rows_hbm, send_rows),
                 (send_count_hbm, send_count),
@@ -326,11 +328,8 @@
     lax.fori_loop(0, blocks, arrange, 0)
 
     def over_chunks(body):
-        def run(part, carry):
-            body(pl.ds(pl.multiple_of(part * chunk, chunk), chunk))
-            return carry
-
-        lax.fori_loop(0, chunks, run, 0)
+        for part in range(chunks):
+            body(pl.ds(part * chunk, chunk))
 
     def batch_part(source):
         def body(rows):

time: 72.7 us -> 69.8 us (0.960)
  Pallas kernels: 71.9 us -> 69 us
    pallas_call x1, Pallas kernels: 69.8 us -> 66.9 us  [local(): pl.pallas_call(functools.partial(step_kernel, grid), out_shape=(jax.Shape...]
where the time goes in v4:
time: 69.8 us; the launch traced here: 69.7 us
  Pallas kernels  69 us (99%)
    pallas_call x1, Pallas kernels, local(): pl.pallas_call(functools.partial(step_kernel, grid), out_shape=(jax.Shape...  66.9 us
    pallas_call x1, Pallas kernels, local(): pl.pallas_call(finish, out_shape=(jax.ShapeDtypeStruct(written.shape, bf1...  2.11 us

profile of v4, /device:TPU:1, one launch (start us, length us, event | category | flops | bytes accessed | tf_op | source)
XLA Modules:
  0.0 69.7 jit_solution(6845032679091173448)
XLA Ops:
  0.6 66.9 %shard_map.95 = (bf16[1,1024,256]{2,1,0:T(8,128)(2,1)}, bf16[512,256]{1,0:T(8,128)(2,1)}) custom-call(bf16[2,1024,256]{2,1,0:T(8,128)(2,1)} %history.1, bf16[64,128,128]{2,1,0:T(8,128)(2,1)} %bitcast.4, s32[8,8]{1,0:T(8,128)} %cols_hbm.1, s32[8,64]{1,0:T(8,128)} %bitcast.5, s32[1,64]{1,0:T(1,128)} %send_count_hbm.1, s32[1,1024]{1,0:T(1,128)} %node_ids_hbm.1, ...), custom_call_target="tpu_custom_call" | custom-call | tf_op jit(solution)/shard_map/pallas_call | solution.py:411
  67.6 2.1 %shard_map.96 = (bf16[1,1024,256]{2,1,0:T(8,128)(2,1)}, f32[2,256,256]{2,1,0:T(8,128)}) custom-call(bf16[1,1024,256]{2,1,0:T(8,128)(2,1)} %get-tuple-element.4.written_ref, bf16[512,256]{1,0:T(8,128)(2,1)} %get-tuple-element.5.total_ref), custom_call_target="tpu_custom_call" | custom-call | tf_op jit(solution)/shard_map/pallas_call | solution.py:461

commit v5 on v4

--- a/solution.py
+++ b/solution.py
@@ -100,12 +100,16 @@
     group = shares // 2
     mine, span, device = layer_share(grid, rows)
 
+    same = jnp.where(mine // group == level, 1, 0)
+
     def send(turn, carry):
-        index = level * group + (mine + turn) % group
+        step = turn + 3
+        step = jnp.where(step >= group - same, step - (group - same), step)
+        index = level * group + (mine + same + step) % group
         link(0, source.at[span(index)], layer_got.at[mine], device(index), send_sems, recv_sems).start()
         return carry
 
-    lax.fori_loop(jnp.where(mine // group == level, 1, 0), group, send, 0)
+    lax.fori_loop(0, group - same, send, 0)
 
 
 def sum_rest(grid, scale, out, source, layer_got, ring_got, send_sems, recv_sems):
@@ -121,7 +125,7 @@
         link(1, ring_got.at[z], ring_got.at[z], ring_peer(grid, turn), send_sems, recv_sems).start()
         return carry
 
-    lax.fori_loop(0, nz - 1, ring_send, 0)
+    lax.fori_loop(0, nz - 1, ring_send, 0, unroll=nz - 1)
     span_wait(source.at[pl.ds(0, (shares - 1) * rows)], send_sems.at[0])
     span_wait(ring_got.at[pl.ds(0, nz - 1)], recv_sems.at[1])
     total = jnp.sum(ring_got[...].astype(jnp.float32), axis=0) * scale
@@ -132,7 +136,7 @@
         link(2, source.at[span(mine)], out.at[span(mine)], device(index), send_sems, recv_sems).start()
         return carry
 
-    lax.fori_loop(0, shares - 1, share, 0)
+    lax.fori_loop(0, shares - 1, share, 0, unroll=shares - 1)
     own = pltpu.make_async_copy(source.at[span(mine)], out.at[span(mine)], send_sems.at[3])
     own.start()
     span_wait(ring_got.at[pl.ds(0, nz - 1)], send_sems.at[1])
@@ -203,6 +207,8 @@
     mixed,
     slope,
     back,
+    mixed_turned,
+    weight_turned,
     send_buf,
     halo_got,
     halo,
@@ -370,6 +376,8 @@
     over_chunks(write_back)
     store = pltpu.make_async_copy(written_rows, written.at[0], local_sems.at[len(loads)])
     store.start()
+    mixed_turned[...] = mixed[0].astype(f32).T.astype(bf16)
+    weight_turned[...] = weights[1].astype(f32).T.astype(bf16)
     loads[8].wait()
     receive(1)
     beta_last = layer_beta(1)
@@ -378,8 +386,7 @@
         z = preact(1, rows)
         grad = (upstream[rows, :].astype(f32) * silu_slope(z)).astype(bf16)
         upstream[rows, :] = grad
-        turned = lax.dot_general(grad, weights[1], (((1,), (1,)), ((), ())), preferred_element_type=f32)
-        back[rows, :] = ((1.0 - beta_last) * grad.astype(f32) + beta_last * turned).astype(bf16)
+        back[rows, :] = ((1.0 - beta_last) * grad.astype(f32) + beta_last * dot(grad, weight_turned[...])).astype(bf16)
 
     over_chunks(last_layer)
     source = sum_refs[0]
@@ -391,7 +398,7 @@
         hidden[rows, :] = ((1.0 - RESTART) * total * slope[rows, :]).astype(bf16)
 
     over_chunks(first_grad)
-    source[:width, :] = (layer_beta(0) * dot_t(mixed[0], hidden[...])).astype(bf16)
+    source[:width, :] = (layer_beta(0) * dot(mixed_turned[...], hidden[...])).astype(bf16)
     sum_send(grid, 0, *sum_refs)
     nodes_all = batch * owners * lax.axis_size("rep")
     sum_rest(grid, 1.0 / math.sqrt(nodes_all), total_out, *sum_refs)
@@ -433,6 +440,8 @@
             pltpu.VMEM((levels, batch, width), bf16),
             pltpu.VMEM((batch, width), f32),
             pltpu.VMEM((batch, width), bf16),
+            pltpu.VMEM((width, batch), bf16),
+            pltpu.VMEM((width, width), bf16),
             pltpu.VMEM((levels, owners, 2 * cap, width // 2), bf16),
             pltpu.VMEM((levels, owners, 2 * cap, width // 2), bf16),
             pltpu.VMEM((slots, width), bf16),

time: 69.8 us -> 69.9 us (level)
  no operation moved by 1% of the time
where the time goes in v5:
time: 69.9 us; the launch traced here: 69.7 us
  Pallas kernels  69.1 us (99%)
    pallas_call x1, Pallas kernels, local(): pl.pallas_call(functools.partial(step_kernel, grid), out_shape=(jax.Shape...  67 us
    pallas_call x1, Pallas kernels, local(): pl.pallas_call(finish, out_shape=(jax.ShapeDtypeStruct(written.shape, bf1...  2.11 us

profile of v5, /device:TPU:1, one launch (start us, length us, event | category | flops | bytes accessed | tf_op | source)
XLA Modules:
  0.0 69.7 jit_solution(2505721355800545781)
XLA Ops:
  0.6 67.0 %shard_map.95 = (bf16[1,1024,256]{2,1,0:T(8,128)(2,1)}, bf16[512,256]{1,0:T(8,128)(2,1)}) custom-call(bf16[2,1024,256]{2,1,0:T(8,128)(2,1)} %history.1, bf16[64,128,128]{2,1,0:T(8,128)(2,1)} %bitcast.4, s32[8,8]{1,0:T(8,128)} %cols_hbm.1, s32[8,64]{1,0:T(8,128)} %bitcast.5, s32[1,64]{1,0:T(1,128)} %send_count_hbm.1, s32[1,1024]{1,0:T(1,128)} %node_ids_hbm.1, ...), custom_call_target="tpu_custom_call" | custom-call | tf_op jit(solution)/shard_map/pallas_call | solution.py:418
  67.6 2.1 %shard_map.96 = (bf16[1,1024,256]{2,1,0:T(8,128)(2,1)}, f32[2,256,256]{2,1,0:T(8,128)}) custom-call(bf16[1,1024,256]{2,1,0:T(8,128)(2,1)} %get-tuple-element.4.written_ref, bf16[512,256]{1,0:T(8,128)(2,1)} %get-tuple-element.5.total_ref), custom_call_target="tpu_custom_call" | custom-call | tf_op jit(solution)/shard_map/pallas_call | solution.py:470

commit v6 on v5

--- a/solution.py
+++ b/solution.py
@@ -116,7 +116,7 @@
     nx, ny, nz = grid
     shares, rows = layer_got.shape[0], layer_got.shape[1]
     mine, span, device = layer_share(grid, rows)
-    z = place(grid)[1]
+    x, z, y, core = place(grid)
     layer_got[mine] = source[span(mine), :]
     span_wait(layer_got.at[pl.ds(0, shares - 1)], recv_sems.at[0])
     ring_got[z] = jnp.sum(layer_got[...].astype(jnp.float32), axis=0).astype(jnp.bfloat16)
@@ -132,7 +132,9 @@
     source[span(mine), :] = total.astype(jnp.bfloat16)
 
     def share(turn, carry):
-        index = (mine + 1 + (shares // 2 + ny - 1 + turn) % (shares - 1)) % shares
+        over_x = (x + far_first(nx, turn // (2 * ny))) % nx
+        over_y = (y + far_first(ny, turn // 2 % ny)) % ny
+        index = (over_x * ny + over_y) * 2 + (core + 1 + turn) % 2
         link(2, source.at[span(mine)], out.at[span(mine)], device(index), send_sems, recv_sems).start()
         return carry
 
@@ -160,10 +162,6 @@
 
 def dot(a, b):
     return jnp.dot(a, b, preferred_element_type=jnp.float32)
-
-
-def dot_t(a, b):
-    return lax.dot_general(a, b, (((0,), (0,)), ((), ())), preferred_element_type=jnp.float32)
 
 
 def iota(shape, axis):
@@ -208,6 +206,7 @@
     slope,
     back,
     mixed_turned,
+    last_turned,
     weight_turned,
     send_buf,
     halo_got,
@@ -384,13 +383,14 @@
 
     def last_layer(rows):
         z = preact(1, rows)
+        last_turned[:, rows] = mixed[1, rows, :].astype(f32).T.astype(bf16)
         grad = (upstream[rows, :].astype(f32) * silu_slope(z)).astype(bf16)
         upstream[rows, :] = grad
         back[rows, :] = ((1.0 - beta_last) * grad.astype(f32) + beta_last * dot(grad, weight_turned[...])).astype(bf16)
 
     over_chunks(last_layer)
     source = sum_refs[0]
-    source[width:, :] = (beta_last * dot_t(mixed[1], upstream[...])).astype(bf16)
+    source[width:, :] = (beta_last * dot(last_turned[...], upstream[...])).astype(bf16)
     sum_send(grid, 1, *sum_refs)
 
     def first_grad(rows):
@@ -441,6 +441,7 @@
             pltpu.VMEM((batch, width), f32),
             pltpu.VMEM((batch, width), bf16),
             pltpu.VMEM((width, batch), bf16),
+            pltpu.VMEM((width, batch), bf16),
             pltpu.VMEM((width, width), bf16),
             pltpu.VMEM((levels, owners, 2 * cap, width // 2), bf16),
             pltpu.VMEM((levels, owners, 2 * cap, width // 2), bf16),

time: 69.9 us -> 69.7 us (level)
  no operation moved by 1% of the time
where the time goes in v6:
time: 69.7 us; the launch traced here: 69.6 us
  Pallas kernels  68.9 us (99%)
    pallas_call x1, Pallas kernels, local(): pl.pallas_call(functools.partial(step_kernel, grid), out_shape=(jax.Shape...  66.8 us
    pallas_call x1, Pallas kernels, local(): pl.pallas_call(finish, out_shape=(jax.ShapeDtypeStruct(written.shape, bf1...  2.11 us

profile of v6, /device:TPU:1, one launch (start us, length us, event | category | flops | bytes accessed | tf_op | source)
XLA Modules:
  0.0 69.6 jit_solution(10398888395049232972)
XLA Ops:
  0.6 66.8 %shard_map.95 = (bf16[1,1024,256]{2,1,0:T(8,128)(2,1)}, bf16[512,256]{1,0:T(8,128)(2,1)}) custom-call(bf16[2,1024,256]{2,1,0:T(8,128)(2,1)} %history.1, bf16[64,128,128]{2,1,0:T(8,128)(2,1)} %bitcast.4, s32[8,8]{1,0:T(8,128)} %cols_hbm.1, s32[8,64]{1,0:T(8,128)} %bitcast.5, s32[1,64]{1,0:T(1,128)} %send_count_hbm.1, s32[1,1024]{1,0:T(1,128)} %node_ids_hbm.1, ...), custom_call_target="tpu_custom_call" | custom-call | tf_op jit(solution)/shard_map/pallas_call | solution.py:418
  67.5 2.1 %shard_map.96 = (bf16[1,1024,256]{2,1,0:T(8,128)(2,1)}, f32[2,256,256]{2,1,0:T(8,128)}) custom-call(bf16[1,1024,256]{2,1,0:T(8,128)(2,1)} %get-tuple-element.4.written_ref, bf16[512,256]{1,0:T(8,128)(2,1)} %get-tuple-element.5.total_ref), custom_call_target="tpu_custom_call" | custom-call | tf_op jit(solution)/shard_map/pallas_call | solution.py:471

commit v7 on v6

--- a/solution.py
+++ b/solution.py
@@ -295,16 +295,16 @@
     for level in range(2):
         loads[2 + level].wait()
         if level == 0:
-            fill(0, 0)
+            lax.fori_loop(0, owners // group, lambda part, carry: (fill(0, part), carry)[1], 0)
             pl.semaphore_wait(barrier, greeted)
-            post(0, 0)
 
         def emit(part, carry):
-            fill(level, part)
+            if level > 0:
+                fill(level, part)
             post(level, part)
             return carry
 
-        lax.fori_loop(1 - level, owners // group, emit, 0)
+        lax.fori_loop(0, owners // group, emit, 0)
         halo_got[level, me] = send_buf[level, owners - 1]
 
     loads[4].wait()

time: 69.7 us -> 69.9 us (level)
  no operation moved by 1% of the time
where the time goes in v7:
time: 69.9 us; the launch traced here: 69.7 us
  Pallas kernels  69.1 us (99%)
    pallas_call x1, Pallas kernels, local(): pl.pallas_call(functools.partial(step_kernel, grid), out_shape=(jax.Shape...  67 us
    pallas_call x1, Pallas kernels, local(): pl.pallas_call(finish, out_shape=(jax.ShapeDtypeStruct(written.shape, bf1...  2.11 us

profile of v7, /device:TPU:1, one launch (start us, length us, event | category | flops | bytes accessed | tf_op | source)
XLA Modules:
  0.0 69.7 jit_solution(5356583391748408708)
XLA Ops:
  0.6 67.0 %shard_map.95 = (bf16[1,1024,256]{2,1,0:T(8,128)(2,1)}, bf16[512,256]{1,0:T(8,128)(2,1)}) custom-call(bf16[2,1024,256]{2,1,0:T(8,128)(2,1)} %history.1, bf16[64,128,128]{2,1,0:T(8,128)(2,1)} %bitcast.4, s32[8,8]{1,0:T(8,128)} %cols_hbm.1, s32[8,64]{1,0:T(8,128)} %bitcast.5, s32[1,64]{1,0:T(1,128)} %send_count_hbm.1, s32[1,1024]{1,0:T(1,128)} %node_ids_hbm.1, ...), custom_call_target="tpu_custom_call" | custom-call | tf_op jit(solution)/shard_map/pallas_call | solution.py:418
  67.6 2.1 %shard_map.96 = (bf16[1,1024,256]{2,1,0:T(8,128)(2,1)}, f32[2,256,256]{2,1,0:T(8,128)}) custom-call(bf16[1,1024,256]{2,1,0:T(8,128)(2,1)} %get-tuple-element.4.written_ref, bf16[512,256]{1,0:T(8,128)(2,1)} %get-tuple-element.5.total_ref), custom_call_target="tpu_custom_call" | custom-call | tf_op jit(solution)/shard_map/pallas_call | solution.py:471
